TPU v7x, 32 devices: a whole 2x2x4 slice. The times are simulated.
32 devices in a mesh: groups: 2 (over x), blk: 16 (over z, y, core).
Axes of the slice: x: 2, y: 2, z: 4, core: 2. Of those that a mesh axis runs over, the one named last changes fastest.
Arguments:
- tokens: bfloat16 [8192, 8192], P(('groups', 'blk')), parts along dimension 0, may hold values from -6 to 6
- shrink_panels: bfloat16 [32, 8192, 64], P(None, 'blk'), may hold values from -0.0625 to 0.0625
- expand_panels: bfloat16 [32, 64, 8192], P(None, None, 'blk'), may hold values from -0.75 to 0.75
- adapter_scale: float32 [32], replicated, may hold values from 0.5 to 2
- block_adapter: int32 [128, 1], P('groups'), parts along dimension 0, may hold values from 0 to 31
- shard_counts: int32 [32], P('groups'), parts along dimension 0, may hold values from 1 to 256, as said below
Outputs:
- update: bfloat16 [8192, 8192], P(('groups', 'blk')), parts along dimension 0
There are 2 independent parts, one for each index of `groups`. A program takes and returns all parts, laid end to end along the dimension named above; an argument that names none is the same for every part. Nothing has to cross between parts.
Inputs may be any that keep to these rules, and one draw needn't show every extreme that they name: `shard_counts`: every shard holds at least one live row; in every draw some shard is full.
All inputs are finite; a program needn't handle non-finite values.
Results may differ from a plain program's by a relative error of at most 0.0049.
Values may be sent and summed in bfloat16 or wider, within the bound.
No kernel may reach another device: no remote copies, remote signals or barrier semaphores. Data moves between devices by JAX's collectives and lax.ppermute only.
A program may use at most 128 MiB of HBM per device.

v0:
```python
import functools

import jax
import jax.numpy as jnp
from jax import lax
from jax.experimental import pallas as pl
from jax.experimental.pallas import tpu as pltpu
from jax.sharding import PartitionSpec as P

BLOCK = 64
ROWS = 16
CAPS = (16, 17, 18, 19, 20, 21, 22, 24, 28, 40)
PLANE = 4
VMEM_BYTES = 60 * 2**20

SMEM = pl.BlockSpec(memory_space=pltpu.SMEM)
VMEM = pl.BlockSpec(memory_space=pltpu.VMEM)
HBM = pl.BlockSpec(memory_space=pl.ANY)


SMALL = pl.CostEstimate(flops=0, bytes_accessed=1024, transcendentals=0)


def prepare_kernel(dims, caps, where, *rest):
    groups, planes, adapters, stride, own = dims
    facts, panels = rest[:groups], rest[groups]
    sent, rest = rest[groups + 1 : groups + 1 + PLANE], rest[groups + 1 + PLANE :]
    lists, bounds, places, last_places, pick, slot, last_slot, last_list, known, sems = rest
    plane_blocks = PLANE * own
    blocks = planes * plane_blocks
    row = blocks + planes * PLANE
    my_plane, my_group, my_shard = where[0], where[1], where[2]

    for t, out in enumerate(sent):
        shard = lax.rem(my_shard + t, PLANE)

        def send(s, carry, out=out, shard=shard, t=t):
            base = (lax.rem(my_plane + s, planes) * PLANE + shard) * own
            for b in range(own - 1):
                pltpu.make_async_copy(panels.at[facts[0][base + b]], out.at[s, b], sems.at[t]).start()
            return carry

        lax.fori_loop(0, planes, send, 0)

    for d, fact in enumerate(facts):
        base = lax.rem(my_group - d + groups, groups) * row

        def keep(i, carry, fact=fact, base=base):
            for k in range(PLANE):
                known[base + i * PLANE + k] = fact[i * PLANE + k]
            return carry

        lax.fori_loop(0, row // PLANE, keep, 0)

    def one_plane(plane, largest):
        at_slot, at_list = plane * adapters, plane * stride

        def clear(i, carry):
            for k in range(8):
                slot[at_slot + i * 8 + k] = -1
                last_slot[at_slot + i * 8 + k] = -1
            return carry

        lax.fori_loop(0, adapters // 8, clear, 0)
        found, last_found = jnp.int32(0), jnp.int32(0)
        for group in range(groups):
            for shard in range(PLANE):
                count = known[group * row + blocks + plane * PLANE + shard]
                for k in range(own):
                    adapter = known[group * row + plane * plane_blocks + shard * own + k]
                    held = slot[at_slot + adapter]
                    new = jnp.logical_and(count > k * BLOCK, held < 0)
                    slot[at_slot + adapter] = jnp.where(new, found, held)
                    lists[at_list + found] = adapter
                    found = found + new.astype(jnp.int32)
                held = last_slot[at_slot + adapter]
                new = jnp.logical_and(count > (own - 1) * BLOCK, held < 0)
                last_slot[at_slot + adapter] = jnp.where(new, last_found, held)
                last_list[last_found] = adapter
                last_found = last_found + new.astype(jnp.int32)

        def append(i, carry):
            lists[at_list + found + i] = last_list[i]
            return carry

        def fill(i, carry):
            lists[at_list + i] = 0
            return carry

        bounds[plane] = found
        lax.fori_loop(0, last_found, append, 0)
        lax.fori_loop(found + last_found, stride, fill, 0)
        return jnp.maximum(largest, found + last_found)

    largest = lax.fori_loop(0, planes, one_plane, jnp.int32(0))
    branch = jnp.int32(0)
    for cap in caps[:-1]:
        branch = branch + (largest > cap).astype(jnp.int32)
    pick[0] = branch

    def one_group(group, carry):
        for block in range(plane_blocks):
            adapter = known[group * row + my_plane * plane_blocks + block]
            places[group * plane_blocks + block] = jnp.maximum(slot[my_plane * adapters + adapter], 0)
            if block % own == own - 1:
                place = bounds[my_plane] + last_slot[my_plane * adapters + adapter]
                last_places[group * PLANE + block // own] = jnp.maximum(place, 0)
        return carry

    lax.fori_loop(0, groups, one_group, 0)
    for t, out in enumerate(sent):
        pltpu.make_async_copy(out, out, sems.at[t]).wait()


def prepare(dims, caps, where, facts, panels):
    groups, planes, adapters, stride, own = dims
    ints = lambda n: jax.ShapeDtypeStruct((n,), jnp.int32)
    sent = jax.ShapeDtypeStruct((planes, own - 1, *panels.shape[1:]), panels.dtype)
    row = planes * PLANE * (own + 1)
    counts = (planes * stride, planes, groups * PLANE * own, groups * PLANE, 1)
    return pl.pallas_call(
        functools.partial(prepare_kernel, dims, caps),
        out_shape=(*(sent,) * PLANE, *map(ints, counts)),
        in_specs=[SMEM, *[SMEM] * groups, VMEM],
        out_specs=(*(HBM,) * PLANE, *(SMEM,) * len(counts)),
        scratch_shapes=[
            pltpu.SMEM((planes * adapters,), jnp.int32),
            pltpu.SMEM((planes * adapters,), jnp.int32),
            pltpu.SMEM((groups * PLANE + 1,), jnp.int32),
            pltpu.SMEM((groups * row,), jnp.int32),
            pltpu.SemaphoreType.DMA((PLANE,)),
        ],
        compiler_params=pltpu.CompilerParams(vmem_limit_bytes=VMEM_BYTES),
        cost_estimate=SMALL,
        name="prepare",
    )(where, *facts, panels)


def regroup_kernel(planes, where, *refs):
    held, out, sem = refs[:PLANE], refs[PLANE], refs[-1]
    for s in range(planes):
        plane = lax.rem(where[0] + s, planes)
        for t in range(PLANE):
            pltpu.make_async_copy(held[t].at[s], out.at[plane, t], sem).start()
    pltpu.make_async_copy(out, out, sem).wait()


def regroup(where, held):
    planes = held[0].shape[0]
    return pl.pallas_call(
        functools.partial(regroup_kernel, planes),
        out_shape=jax.ShapeDtypeStruct((planes, PLANE, *held[0].shape[1:]), held[0].dtype),
        in_specs=[SMEM, *[VMEM] * PLANE],
        out_specs=HBM,
        scratch_shapes=[pltpu.SemaphoreType.DMA],
        compiler_params=pltpu.CompilerParams(vmem_limit_bytes=VMEM_BYTES),
        cost_estimate=SMALL,
        name="regroup",
    )(where, *held)


def plane_pack_kernel(dims, first, where, lists, bounds, panels, last_panels, *rest):
    groups, planes, adapters, stride, own = dims
    outs, (held, last_held, held_sems, sems) = rest[:-4], rest[-4:]
    share = outs[0].shape[1]
    mine = pl.ds(pl.multiple_of(first + where[1] * share, share), share)
    loads = [
        pltpu.make_async_copy(panels.at[:, mine], held, held_sems.at[0]),
        pltpu.make_async_copy(last_panels.at[:, mine], last_held, held_sems.at[1]),
    ]
    for load in loads:
        load.start()
    for load in loads:
        load.wait()
    for i, out in enumerate(outs):
        plane = lax.rem(where[0] + i + 1, planes)

        def send(k, carry, out=out, plane=plane, i=i):
            pltpu.make_async_copy(held.at[lists[plane * stride + k]], out.at[k], sems.at[i]).start()
            return carry

        def send_last(k, carry, out=out, plane=plane, i=i):
            pltpu.make_async_copy(last_held.at[lists[plane * stride + k]], out.at[k], sems.at[i]).start()
            return carry

        lax.fori_loop(0, bounds[plane], send, 0)
        lax.fori_loop(bounds[plane], out.shape[0], send_last, 0)
    for i, out in enumerate(outs):
        pltpu.make_async_copy(out, out, sems.at[i]).wait()


def plane_pack(dims, cap, first, ranks, where, lists, bounds, panels, last_panels):
    groups, planes = dims[:2]
    out = jax.ShapeDtypeStruct((cap, ranks // groups, panels.shape[2]), panels.dtype)
    return pl.pallas_call(
        functools.partial(plane_pack_kernel, dims, first),
        out_shape=(out,) * (planes - 1),
        in_specs=[SMEM, SMEM, SMEM, HBM, HBM],
        out_specs=(HBM,) * (planes - 1),
        scratch_shapes=[
            pltpu.VMEM((panels.shape[0], *out.shape[1:]), panels.dtype),
            pltpu.VMEM((panels.shape[0], *out.shape[1:]), panels.dtype),
            pltpu.SemaphoreType.DMA((2,)),
            pltpu.SemaphoreType.DMA((planes - 1,)),
        ],
        compiler_params=pltpu.CompilerParams(vmem_limit_bytes=VMEM_BYTES),
        cost_estimate=SMALL,
        name="plane_pack",
    )(where, lists, bounds, panels, last_panels)


def group_pack_kernel(dims, where, places, last_places, *rest):
    groups, planes, adapters, stride, own = dims
    got, outs, sems = rest[: planes - 1], rest[planes - 1 : -1], rest[-1]
    blocks = PLANE * own
    for i, out in enumerate(outs):
        group = lax.rem(where[1] + i + 1, groups)

        def send(j, place, out=out, i=i):
            for s in range(planes - 1):
                pltpu.make_async_copy(got[s].at[place], out.at[j, s], sems.at[i]).start()

        def send_block(j, carry, send=send, group=group):
            send(j, places[group * blocks + j])
            return carry

        lax.fori_loop(0, blocks, send_block, 0)
        for shard in range(PLANE):
            send(blocks + shard, last_places[group * PLANE + shard])
    for i, out in enumerate(outs):
        pltpu.make_async_copy(out, out, sems.at[i]).wait()


def group_pack(dims, where, places, last_places, got):
    groups, planes, adapters, stride, own = dims
    out = jax.ShapeDtypeStruct((PLANE * (own + 1), planes - 1, *got[0].shape[1:]), got[0].dtype)
    return pl.pallas_call(
        functools.partial(group_pack_kernel, dims),
        out_shape=(out,) * (groups - 1),
        in_specs=[SMEM, SMEM, SMEM, *[VMEM] * (planes - 1)],
        out_specs=(HBM,) * (groups - 1),
        scratch_shapes=[pltpu.SemaphoreType.DMA((groups - 1,))],
        compiler_params=pltpu.CompilerParams(vmem_limit_bytes=VMEM_BYTES),
        cost_estimate=SMALL,
        name="group_pack",
    )(where, places, last_places, *got)


def shard_pack_kernel(dims, first, where, places, last_places, ids, panels, last_panels, *rest):
    groups, planes, adapters, stride, own = dims
    got = rest[: planes - 1]
    swapped = rest[planes - 1 : planes + groups - 2]
    outs, sems = rest[planes + groups - 2 : -1], rest[-1]
    ranks, share = outs[0].shape[2], got[0].shape[1]
    my_group, my_shard = where[1], where[2]

    def part(group):
        return pl.ds(pl.multiple_of(group * share, share), share)

    for t, out in enumerate(outs):
        shard = lax.rem(my_shard + t, PLANE)

        def send(b, source, place, behind, out=out, t=t):
            copy = lambda src, dst: pltpu.make_async_copy(src, dst, sems.at[t]).start()
            copy(source.at[pl.ds(first, ranks)], out.at[b, 0])
            for s in range(planes - 1):
                copy(got[s].at[place], out.at[b, s + 1, part(my_group)])
            for d in range(groups - 1):
                other = lax.rem(my_group + groups - d - 1, groups)
                copy(swapped[d].at[behind], out.at[b, pl.ds(1, planes - 1), part(other)])

        def send_block(b, carry, send=send, shard=shard):
            j = shard * own + b
            send(b, panels.at[ids[j]], places[my_group * PLANE * own + j], j)
            return carry

        lax.fori_loop(0, own, send_block, 0)
        last = last_panels.at[ids[shard * own + own - 1]]
        send(own, last, last_places[my_group * PLANE + shard], PLANE * own + shard)
    for t, out in enumerate(outs):
        pltpu.make_async_copy(out, out, sems.at[t]).wait()


def shard_pack(dims, first, ranks, where, places, last_places, ids, panels, last_panels, got, swapped):
    groups, planes, adapters, stride, own = dims
    out = jax.ShapeDtypeStruct((own + 1, planes, ranks, panels.shape[2]), panels.dtype)
    return pl.pallas_call(
        functools.partial(shard_pack_kernel, dims, first),
        out_shape=(out,) * PLANE,
        in_specs=[*[SMEM] * 4, VMEM, VMEM, *[VMEM] * (planes + groups - 2)],
        out_specs=(HBM,) * PLANE,
        scratch_shapes=[pltpu.SemaphoreType.DMA((PLANE,))],
        compiler_params=pltpu.CompilerParams(vmem_limit_bytes=VMEM_BYTES),
        cost_estimate=SMALL,
        name="shard_pack",
    )(where, places, last_places, ids, panels, last_panels, *got, *swapped)


def shrink_kernel(planes, where, tokens, *rest):
    maps, out = rest[:-1], rest[-1]
    width = maps[0].shape[-1]
    total = jnp.zeros(out.shape, jnp.float32)
    for t in range(PLANE):
        shard = lax.rem(where[2] + PLANE - t, PLANE)
        for s in range(planes):
            source = lax.rem(where[0] + planes - s, planes) * PLANE + shard
            total += lax.dot_general(
                tokens[:, pl.ds(pl.multiple_of(source * width, width), width)],
                jnp.concatenate([m[0, s] for m in maps[t::PLANE]], axis=0),
                (((1,), (1,)), ((), ())),
                preferred_element_type=jnp.float32,
            )
    out[...] = total.astype(out.dtype)


def shrink(where, tokens, maps):
    own, (planes, ranks, width) = tokens.shape[0] // BLOCK, maps[0].shape[1:]
    rank = len(maps) // PLANE * ranks
    return pl.pallas_call(
        functools.partial(shrink_kernel, planes),
        grid=(own,),
        out_shape=jax.ShapeDtypeStruct((own * BLOCK, rank), tokens.dtype),
        in_specs=[
            SMEM,
            pl.BlockSpec((BLOCK, tokens.shape[1]), lambda b: (b, 0)),
            *[pl.BlockSpec((1, planes, ranks, width), lambda b: (b, 0, 0, 0))] * len(maps),
        ],
        out_specs=pl.BlockSpec((BLOCK, rank), lambda b: (b, 0)),
        compiler_params=pltpu.CompilerParams(vmem_limit_bytes=VMEM_BYTES),
        cost_estimate=SMALL,
        name="shrink",
    )(where, tokens, *maps)


def expand_kernel(where, ids, count, scales, shrunk, direct, *rest):
    last, out = rest[:-1], rest[-1]
    b = pl.program_id(0)
    scale = scales[ids[b]]
    planes, width = direct.shape[0], direct.shape[-1]
    rows = b * BLOCK + lax.broadcasted_iota(jnp.int32, (BLOCK, width), 0)
    live = rows < count[0]

    def write(plane, t, panel):
        source = plane * PLANE + lax.rem(where[2] + PLANE - t, PLANE)
        part = jnp.dot(shrunk[...], panel, preferred_element_type=jnp.float32)
        columns = pl.ds(pl.multiple_of(source * width, width), width)
        out[:, columns] = jnp.where(live, part * scale, 0.0).astype(out.dtype)

    @pl.when(b < pl.num_programs(0) - 1)
    def _():
        for plane in range(planes):
            for t in range(PLANE):
                write(plane, t, direct[plane, t, 0])

    @pl.when(b == pl.num_programs(0) - 1)
    def _():
        for s in range(planes):
            for t in range(PLANE):
                panel = jnp.concatenate([m[0, s] for m in last[t::PLANE]], axis=0)
                write(lax.rem(where[0] + planes - s, planes), t, panel)


def expand(where, ids, count, scales, shrunk, direct, maps):
    planes, _, blocks, rank, width = direct.shape
    own, ranks = blocks + 1, maps[0].shape[2]
    columns = planes * PLANE * width
    return pl.pallas_call(
        expand_kernel,
        grid=(own,),
        out_shape=jax.ShapeDtypeStruct((own * BLOCK, columns), shrunk.dtype),
        in_specs=[
            *[SMEM] * 4,
            pl.BlockSpec((BLOCK, rank), lambda b: (b, 0)),
            pl.BlockSpec((planes, PLANE, 1, rank, width), lambda b: (0, 0, jnp.minimum(b, blocks - 1), 0, 0)),
            *[pl.BlockSpec((1, planes, ranks, width), lambda b: (own, 0, 0, 0))] * len(maps),
        ],
        out_specs=pl.BlockSpec((BLOCK, columns), lambda b: (b, 0)),
        compiler_params=pltpu.CompilerParams(vmem_limit_bytes=VMEM_BYTES),
        cost_estimate=SMALL,
        name="expand",
    )(where, ids, count, scales, shrunk, direct, *maps)


def body(groups, tokens, shrink_panels, expand_panels, adapter_scale, block_adapter, shard_counts):
    devices = shard_counts.shape[0]
    own = tokens.shape[0] // BLOCK
    planes = devices // PLANE
    adapters = shrink_panels.shape[0]
    most = min(adapters, groups * PLANE * own)
    last_most = min(adapters, groups * PLANE)
    most += last_most
    dims = (groups, planes, adapters, most + 1, own)
    caps = tuple(most * part // CAPS[-1] for part in CAPS)

    ids = block_adapter.reshape(-1)
    me, group = lax.axis_index("blk"), lax.axis_index("groups")
    where = jnp.stack([me // PLANE, group, lax.rem(me, PLANE)]).astype(jnp.int32)
    facts = jnp.concatenate([ids, shard_counts])
    known = [facts]
    for d in range(1, groups):
        known.append(lax.ppermute(facts, "groups", [(i, (i + d) % groups) for i in range(groups)]))
    *up_sent, lists, bounds, places, last_places, pick = prepare(dims, caps, where, known, expand_panels)
    plane_ids = lax.dynamic_slice_in_dim(ids, me // PLANE * PLANE * own, PLANE * own, 0)
    mine = lax.dynamic_slice_in_dim(ids, me * own, own, 0)
    count = lax.dynamic_slice_in_dim(shard_counts, me, 1, 0)
    down_panels = jnp.swapaxes(shrink_panels, 1, 2)

    def plane_shift(x, s):
        return lax.ppermute(x, "blk", [(i, (i + s * PLANE) % devices) for i in range(devices)])

    def group_shift(x, d):
        return lax.ppermute(x, "groups", [(i, (i + d) % groups) for i in range(groups)])

    def shard_shift(x, t):
        pairs = [(i, i // PLANE * PLANE + (i + t) % PLANE) for i in range(devices)]
        return lax.ppermute(x, "blk", pairs)

    rank = expand_panels.shape[1]
    parts = 2 if rank % (2 * groups * ROWS) == 0 else 1
    ranks = rank // parts
    panels = (down_panels, expand_panels)

    def run(cap):
        def branch(up_sent):
            sent = [
                plane_pack(dims, cap, h * ranks, ranks, where, lists, bounds, *panels) for h in range(parts)
            ]
            near = [up_sent[0], *[shard_shift(up_sent[t], t) for t in range(1, PLANE)]]
            up_packed = regroup(where, near)
            got, maps = [], []
            for h in range(parts):
                got.append([plane_shift(x, s + 1) for s, x in enumerate(sent[h])])
                if h + 1 < parts:
                    got[h], sent[h + 1] = lax.optimization_barrier((got[h], sent[h + 1]))
                else:
                    got[h], maps, up_packed = lax.optimization_barrier((got[h], maps, up_packed))
                swaps = group_pack(dims, where, places, last_places, got[h])
                swapped = [group_shift(x, d + 1) for d, x in enumerate(swaps)]
                maps.append(
                    shard_pack(
                        dims, h * ranks, ranks, where, places, last_places, plane_ids, *panels, got[h], swapped
                    )
                )
            mirrors = [list(range(i, devices, PLANE)) for i in range(PLANE)]
            up = lax.all_to_all(up_packed, "blk", split_axis=0, concat_axis=0, tiled=True, axis_index_groups=mirrors)
            routed = []
            for kept, *moved in maps:
                routed += [kept, *[shard_shift(x, t + 1) for t, x in enumerate(moved)]]
            shrunk = shrink(where, tokens, routed)
            return expand(where, mine, count, adapter_scale, shrunk, up, routed)

        return branch

    return lax.switch(pick[0], [run(cap) for cap in caps], up_sent)


def solution(mesh):
    return jax.shard_map(
        functools.partial(body, mesh.shape["groups"]),
        mesh=mesh,
        in_specs=(
            P(("groups", "blk"), None),
            P(None, "blk", None),
            P(None, None, "blk"),
            P(),
            P("groups", None),
            P("groups"),
        ),
        out_specs=P(("groups", "blk"), None),
        check_vma=False,
    )
```

profile of v0, /device:TPU:0, one launch (start us, length us, event | category | flops | bytes accessed | tf_op | source)
XLA Modules:
  0.0 168.2 jit_solution(5549600413113751268)
XLA Ops:
  0.7 2.9 %collective-permute-start.170 = (s32[80]{0:T(128)S(1)}, s32[80]{0:T(128)S(1)}, u32[]{:S(2)}, u32[]{:S(2)}) collective-permute-start(s32[80]{0:T(128)S(1)} %pad_add_fusion.1.rest_0_), channel_id=1, source_target_pairs={{0,16},{16,0},{1,17},{17,1},{2,18},{18,2},{3,19},{19,3},{4,20},{20... | collective-permute-start | bytes 968 | tf_op jit(solution)/shard_map/ppermute | solution.py:401
  5.7 5.8 %prepare.1 = (bf16[4,3,64,512]{3,2,1,0:T(8,128)(2,1)S(1)}, bf16[4,3,64,512]{3,2,1,0:T(8,128)(2,1)}, bf16[4,3,64,512]{3,2,1,0:T(8,128)(2,1)}, bf16[4,3,64,512]{3,...) custom-call(s32[3]{0:T(128)S(1)} %pad_add_fusion.where, ...), custom_call_target="tpu_custom_call" | custom-call | bytes 1024 | tf_op jit(solution)/shard_map/prepare/pallas_call | solution.py:121
  12.2 155.9 %conditional.1 = (bf16[256,8192]{1,0:T(8,128)(2,1)}) conditional(s32[]{:T(128)} %bitcast.24, (s32[3]{0:T(128)S(1)}, s32[164]{0:T(256)S(1)}, s32[4]{0:T(128)S(1)}, bf16[32,64,512]{2,1,0:T(8,128)(2,1)}, bf16[32,64,512]{2,1,0:T(8,128)(2,1)}, /*index=5*/s32[32]{0:T(128)S(1)}, s32[8]{0:T(128)S(1)}, s32[64,1]{0,1:T(1,128)}, ...), branch_computations={%region_0.1_spmd, %region_1.2_spmd, %region_2.3_spmd, %region_3.4_... | conditional | flops 8 | bytes 84947056 | solution.py:454
  12.4 2.8 %plane_pack.32 = (bf16[22,16,512]{2,1,0:T(8,128)(2,1)}, bf16[22,16,512]{2,1,0:T(8,128)(2,1)}, bf16[22,16,512]{2,1,0:T(8,128)(2,1)}) custom-call(s32[3]{0:T(128)S(1)} %get-tuple-element.600.where, s32[164]{0:T(256)S(1)} %get-tuple-element.605.lists, s32[4]{0:T(128)S(1)} %get-tuple-element.606.bounds, bf16[32,64,512]{2,1,0:T(8,128)(2,1)} %get-tuple-element.607.panels, ...), custom_call_target="tpu_custom_call" | custom-call | bytes 1024 | tf_op jit(solution)/shard_map/cond/branch_6_fun/plane_pack/pallas_call | solution.py:195
  15.3 2.2 %collective-permute-start.102 = (bf16[22,16,512]{2,1,0:T(8,128)(2,1)}, bf16[22,16,512]{2,1,0:T(8,128)(2,1)S(1)}, u32[]{:S(2)}, u32[]{:S(2)}) collective-permute-start(bf16[22,16,512]{2,1,0:T(8,128)(2,1)} %get-tuple-element.609), channel_id=1, source_target_pairs={{0,4},{1,5},{2,6},{3,7},{4,8},{5,9},{6,10},{7,11},{8,12},{9,13},{1... | collective-permute-start | bytes 1081352 | tf_op jit(solution)/shard_map/cond/branch_6_fun/ppermute | solution.py:409
  17.4 2.6 %collective-permute-start.103 = (bf16[22,16,512]{2,1,0:T(8,128)(2,1)}, bf16[22,16,512]{2,1,0:T(8,128)(2,1)S(1)}, u32[]{:S(2)}, u32[]{:S(2)}) collective-permute-start(bf16[22,16,512]{2,1,0:T(8,128)(2,1)} %get-tuple-element.610), channel_id=1, source_target_pairs={{0,8},{1,9},{2,10},{3,11},{4,12},{5,13},{6,14},{7,15},{8,0},{9,1},... | collective-permute-start | bytes 1081352 | tf_op jit(solution)/shard_map/cond/branch_6_fun/ppermute | solution.py:409
  22.9 2.6 %plane_pack.33 = (bf16[22,16,512]{2,1,0:T(8,128)(2,1)}, bf16[22,16,512]{2,1,0:T(8,128)(2,1)}, bf16[22,16,512]{2,1,0:T(8,128)(2,1)}) custom-call(s32[3]{0:T(128)S(1)} %get-tuple-element.600.where, s32[164]{0:T(256)S(1)} %get-tuple-element.605.lists, s32[4]{0:T(128)S(1)} %get-tuple-element.606.bounds, bf16[32,64,512]{2,1,0:T(8,128)(2,1)} %get-tuple-element.607.panels, ...), custom_call_target="tpu_custom_call" | custom-call | bytes 1024 | tf_op jit(solution)/shard_map/cond/branch_6_fun/plane_pack/pallas_call | solution.py:195
  25.6 3.5 %collective-permute-done.102.rest_0_ = bf16[22,16,512]{2,1,0:T(8,128)(2,1)S(1)} collective-permute-done((bf16[22,16,512]{2,1,0:T(8,128)(2,1)}, bf16[22,16,512]{2,1,0:T(8,128)(2,1)S(1)}, u32[]{:S(2)}, u32[]{:S(2)}) %collective-permute-start.102) | collective-permute-done | bytes 360480 | tf_op jit(solution)/shard_map/cond/branch_6_fun/ppermute | solution.py:409
  29.1 13.4 %collective-permute-done.103.rest_1_ = bf16[22,16,512]{2,1,0:T(8,128)(2,1)S(1)} collective-permute-done((bf16[22,16,512]{2,1,0:T(8,128)(2,1)}, bf16[22,16,512]{2,1,0:T(8,128)(2,1)S(1)}, u32[]{:S(2)}, u32[]{:S(2)}) %collective-permute-start.103) | collective-permute-done | bytes 360480 | tf_op jit(solution)/shard_map/cond/branch_6_fun/ppermute | solution.py:409
  43.3 2.2 %group_pack.32 = bf16[20,3,16,512]{3,2,1,0:T(8,128)(2,1)} custom-call(s32[3]{0:T(128)S(1)} %get-tuple-element.600.where, s32[32]{0:T(128)S(1)} %get-tuple-element.618.places, s32[8]{0:T(128)S(1)} %get-tuple-element.619.last_places, bf16[22,16,512]{2,1,0:T(8,128)(2,1)} %copy-done.69, bf16[22,16,512]{2,1,0:T(8,128)(2,1)} %copy-done.70, ...), custom_call_target="tpu_custom_call" | custom-call | bytes 1024 | tf_op jit(solution)/shard_map/cond/branch_6_fun/group_pack/pallas_call | solution.py:237
  47.8 7.7 %collective-permute-start.105 = (bf16[22,16,512]{2,1,0:T(8,128)(2,1)}, bf16[22,16,512]{2,1,0:T(8,128)(2,1)S(1)}, u32[]{:S(2)}, u32[]{:S(2)}) collective-permute-start(bf16[22,16,512]{2,1,0:T(8,128)(2,1)} %get-tuple-element.615), channel_id=1, source_target_pairs={{0,4},{1,5},{2,6},{3,7},{4,8},{5,9},{6,10},{7,11},{8,12},{9,13},{1... | collective-permute-start | bytes 1081352 | tf_op jit(solution)/shard_map/cond/branch_6_fun/ppermute | solution.py:409
  58.4 3.3 %regroup.16 = bf16[4,4,3,64,512]{4,3,2,1,0:T(8,128)(2,1)} custom-call(s32[3]{0:T(128)S(1)} %get-tuple-element.600.where, bf16[4,3,64,512]{3,2,1,0:T(8,128)(2,1)S(1)} %get-tuple-element.628.refs_0_, bf16[4,3,64,512]{3,2,1,0:T(8,128)(2,1)} %collective-permute-done.109.refs_1_, bf16[4,3,64,512]{3,2,1,0:T(8,128)(2,1)} %collective-permute-done.110.refs_2_, ...), custom_call_target="tpu_custom_call" | custom-call | bytes 1024 | tf_op jit(solution)/shard_map/cond/branch_6_fun/regroup/pallas_call | solution.py:150
  61.7 7.7 %collective-permute-done.108.rest_3_ = bf16[20,3,16,512]{3,2,1,0:T(8,128)(2,1)} collective-permute-done((bf16[20,3,16,512]{3,2,1,0:T(8,128)(2,1)}, bf16[20,3,16,512]{3,2,1,0:T(8,128)(2,1)}, u32[]{:S(2)}, u32[]{:S(2)}) %collective-permute-start.108) | collective-permute-done | bytes 983072 | tf_op jit(solution)/shard_map/cond/branch_6_fun/ppermute | solution.py:412
  69.4 3.7 %shard_pack.32 = (bf16[5,4,32,512]{3,2,1,0:T(8,128)(2,1)}, bf16[5,4,32,512]{3,2,1,0:T(8,128)(2,1)}, bf16[5,4,32,512]{3,2,1,0:T(8,128)(2,1)}, bf16[5,4,32,512]{3,2,1,0:T(8,128)(2,1)}) custom-call(s32[3]{0:T(128)S(1)} %get-tuple-element.600.where, s32[32]{0:T(128)S(1)} %get-tuple-element.618.places, s32[8]{0:T(128)S(1)} %get-tuple-element.619.last_places, ...), custom_call_target="tpu_custom_call" | custom-call | bytes 1024 | tf_op jit(solution)/shard_map/cond/branch_6_fun/shard_pack/pallas_call | solution.py:287
  73.2 8.1 %collective-permute-done.106.rest_1_ = bf16[22,16,512]{2,1,0:T(8,128)(2,1)} collective-permute-done((bf16[22,16,512]{2,1,0:T(8,128)(2,1)}, bf16[22,16,512]{2,1,0:T(8,128)(2,1)}, u32[]{:S(2)}, u32[]{:S(2)}) %collective-permute-start.106) | collective-permute-done | bytes 360480 | tf_op jit(solution)/shard_map/cond/branch_6_fun/ppermute | solution.py:409
  81.2 9.6 %all-to-all-start.6 = ((bf16[4,4,3,64,512]{4,3,2,1,0:T(8,128)(2,1)}), bf16[4,4,3,64,512]{4,3,2,1,0:T(8,128)(2,1)}, u32[]{:S(2)}, u32[]{:S(2)}) async-start(bf16[4,4,3,64,512]{4,3,2,1,0:T(8,128)(2,1)} %regroup.16), calls=%async_computation.6 | async-start | bytes 6291456 | tf_op jit(solution)/shard_map/cond/branch_6_fun/all_to_all | solution.py:445
  90.8 2.2 %group_pack.33 = bf16[20,3,16,512]{3,2,1,0:T(8,128)(2,1)} custom-call(s32[3]{0:T(128)S(1)} %get-tuple-element.600.where, s32[32]{0:T(128)S(1)} %get-tuple-element.618.places, s32[8]{0:T(128)S(1)} %get-tuple-element.619.last_places, bf16[22,16,512]{2,1,0:T(8,128)(2,1)} %copy-done.68, bf16[22,16,512]{2,1,0:T(8,128)(2,1)} %collective-permute-done.106.rest_1_, ...), custom_call_target="tpu_custom_call" | custom-call | bytes 1024 | tf_op jit(solution)/shard_map/cond/branch_6_fun/group_pack/pallas_call | solution.py:237
  96.6 20.1 %collective-permute-done.115.rest_3_ = bf16[20,3,16,512]{3,2,1,0:T(8,128)(2,1)} collective-permute-done((bf16[20,3,16,512]{3,2,1,0:T(8,128)(2,1)}, bf16[20,3,16,512]{3,2,1,0:T(8,128)(2,1)}, u32[]{:S(2)}, u32[]{:S(2)}) %collective-permute-start.115) | collective-permute-done | bytes 983072 | tf_op jit(solution)/shard_map/cond/branch_6_fun/ppermute | solution.py:412
  116.7 3.7 %shard_pack.33 = (bf16[5,4,32,512]{3,2,1,0:T(8,128)(2,1)}, bf16[5,4,32,512]{3,2,1,0:T(8,128)(2,1)}, bf16[5,4,32,512]{3,2,1,0:T(8,128)(2,1)}, bf16[5,4,32,512]{3,2,1,0:T(8,128)(2,1)}) custom-call(s32[3]{0:T(128)S(1)} %get-tuple-element.600.where, s32[32]{0:T(128)S(1)} %get-tuple-element.618.places, s32[8]{0:T(128)S(1)} %get-tuple-element.619.last_places, ...), custom_call_target="tpu_custom_call" | custom-call | bytes 1024 | tf_op jit(solution)/shard_map/cond/branch_6_fun/shard_pack/pallas_call | solution.py:287
  124.6 13.8 %collective-permute-done.116.rest_5_ = bf16[5,4,32,512]{3,2,1,0:T(8,128)(2,1)S(1)} collective-permute-done((bf16[5,4,32,512]{3,2,1,0:T(8,128)(2,1)}, bf16[5,4,32,512]{3,2,1,0:T(8,128)(2,1)S(1)}, u32[]{:S(2)}, u32[]{:S(2)}) %collective-permute-start.116) | collective-permute-done | bytes 655392 | tf_op jit(solution)/shard_map/cond/branch_6_fun/ppermute | solution.py:416
  139.5 12.6 %collective-permute-done.118.rest_7_ = bf16[5,4,32,512]{3,2,1,0:T(8,128)(2,1)S(1)} collective-permute-done((bf16[5,4,32,512]{3,2,1,0:T(8,128)(2,1)}, bf16[5,4,32,512]{3,2,1,0:T(8,128)(2,1)S(1)}, u32[]{:S(2)}, u32[]{:S(2)}) %collective-permute-start.118) | collective-permute-done | bytes 655392 | tf_op jit(solution)/shard_map/cond/branch_6_fun/ppermute | solution.py:416
  153.0 5.4 %shrink.16.shrunk = bf16[256,64]{1,0:T(8,128)(2,1)} custom-call(s32[3]{0:T(128)S(1)} %get-tuple-element.600.where, bf16[256,8192]{1,0:T(8,128)(2,1)} %get-tuple-element.891.tokens, bf16[5,4,32,512]{3,2,1,0:T(8,128)(2,1)} %get-tuple-element.632.rest_0_, bf16[5,4,32,512]{3,2,1,0:T(8,128)(2,1)} %copy-done.16, bf16[5,4,32,512]{3,2,1,0:T(8,128)(2,1)} %copy-done.26, ...), custom_call_target="tpu_custom_call" | custom-call | bytes 1024 | tf_op jit(solution)/shard_map/cond/branch_6_fun/shrink/pallas_call | solution.py:319
  158.4 3.3 %all-to-all-done.6.direct = bf16[4,4,3,64,512]{4,3,2,1,0:T(8,128)(2,1)} async-done(((bf16[4,4,3,64,512]{4,3,2,1,0:T(8,128)(2,1)}), bf16[4,4,3,64,512]{4,3,2,1,0:T(8,128)(2,1)}, u32[]{:S(2)}, u32[]{:S(2)}) %all-to-all-start.6) | async-done | bytes 3145760 | tf_op jit(solution)/shard_map/cond/branch_6_fun/all_to_all | solution.py:445
  161.6 6.4 %expand.16 = bf16[256,8192]{1,0:T(8,128)(2,1)} custom-call(s32[3]{0:T(128)S(1)} %get-tuple-element.600.where, s32[4]{0:T(128)} %fusion.12.ids, s32[1]{0:T(128)} %dynamic_slice.44.count, f32[32]{0:T(128)S(1)} %copy-done.110, bf16[256,64]{1,0:T(8,128)(2,1)} %shrink.16.shrunk, bf16[4,4,3,64,512]{4,3,2,1,0:T(8,128)(2,1)} %all-to-all-done.6.direct, ...), custom_call_target="tpu_custom_call" | custom-call | bytes 1024 | tf_op jit(solution)/shard_map/cond/branch_6_fun/expand/pallas_call | solution.py:367
  (60 shorter events, 21.5 us)
Async XLA Ops:
  0.7 4.5 %collective-permute-start.170 = (s32[80]{0:T(128)S(1)}, s32[80]{0:T(128)S(1)}, u32[]{:S(2)}, u32[]{:S(2)}) collective-permute-start(s32[80]{0:T(128)S(1)} %pad_add_fusion.1.rest_0_), channel_id=1, source_target_pairs={{0,16},{16,0},{1,17},{17,1},{2,18},{18,2},{3,19},{19,3},{4,20},{20... | collective-permute-start | bytes 968 | tf_op jit(solution)/shard_map/ppermute | solution.py:401
  15.3 13.8 %collective-permute-start.102 = (bf16[22,16,512]{2,1,0:T(8,128)(2,1)}, bf16[22,16,512]{2,1,0:T(8,128)(2,1)S(1)}, u32[]{:S(2)}, u32[]{:S(2)}) collective-permute-start(bf16[22,16,512]{2,1,0:T(8,128)(2,1)} %get-tuple-element.609), channel_id=1, source_target_pairs={{0,4},{1,5},{2,6},{3,7},{4,8},{5,9},{6,10},{7,11},{8,12},{9,13},{1... | collective-permute-start | bytes 1081352 | tf_op jit(solution)/shard_map/cond/branch_6_fun/ppermute | solution.py:409
  17.4 25.1 %collective-permute-start.103 = (bf16[22,16,512]{2,1,0:T(8,128)(2,1)}, bf16[22,16,512]{2,1,0:T(8,128)(2,1)S(1)}, u32[]{:S(2)}, u32[]{:S(2)}) collective-permute-start(bf16[22,16,512]{2,1,0:T(8,128)(2,1)} %get-tuple-element.610), channel_id=1, source_target_pairs={{0,8},{1,9},{2,10},{3,11},{4,12},{5,13},{6,14},{7,15},{8,0},{9,1},... | collective-permute-start | bytes 1081352 | tf_op jit(solution)/shard_map/cond/branch_6_fun/ppermute | solution.py:409
  20.0 22.5 %collective-permute-start.104 = (bf16[22,16,512]{2,1,0:T(8,128)(2,1)}, bf16[22,16,512]{2,1,0:T(8,128)(2,1)}, u32[]{:S(2)}, u32[]{:S(2)}) collective-permute-start(bf16[22,16,512]{2,1,0:T(8,128)(2,1)} %get-tuple-element.611), channel_id=1, source_target_pairs={{0,12},{1,13},{2,14},{3,15},{4,0},{5,1},{6,2},{7,3},{8,4},{9,5},{1... | collective-permute-start | bytes 1081352 | tf_op jit(solution)/shard_map/cond/branch_6_fun/ppermute | solution.py:409
  21.4 34.1 %collective-permute-start.109 = (bf16[4,3,64,512]{3,2,1,0:T(8,128)(2,1)}, bf16[4,3,64,512]{3,2,1,0:T(8,128)(2,1)}, u32[]{:S(2)}, u32[]{:S(2)}) collective-permute-start(bf16[4,3,64,512]{3,2,1,0:T(8,128)(2,1)} %get-tuple-element.629), channel_id=1, source_target_pairs={{0,1},{1,2},{2,3},{3,0},{4,5},{5,6},{6,7},{7,4},{8,9},{9,10},{10,1... | collective-permute-start | bytes 2359304 | tf_op jit(solution)/shard_map/cond/branch_6_fun/ppermute | solution.py:416
  21.4 36.4 %copy-start.137 = (s32[64,1]{0,1:T(1,128)S(1)}, s32[64,1]{0,1:T(1,128)}, u32[]{:S(2)}) copy-start(s32[64,1]{0,1:T(1,128)} %get-tuple-element.913) | copy-start | bytes 772 | tf_op jit(solution)/shard_map/cond
  21.4 35.4 %collective-permute-start.110 = (bf16[4,3,64,512]{3,2,1,0:T(8,128)(2,1)}, bf16[4,3,64,512]{3,2,1,0:T(8,128)(2,1)}, u32[]{:S(2)}, u32[]{:S(2)}) collective-permute-start(bf16[4,3,64,512]{3,2,1,0:T(8,128)(2,1)} %get-tuple-element.630), channel_id=1, source_target_pairs={{0,2},{1,3},{2,0},{3,1},{4,6},{5,7},{6,4},{7,5},{8,10},{9,11},{10,... | collective-permute-start | bytes 2359304 | tf_op jit(solution)/shard_map/cond/branch_6_fun/ppermute | solution.py:416
  45.5 24.0 %collective-permute-start.108 = (bf16[20,3,16,512]{3,2,1,0:T(8,128)(2,1)}, bf16[20,3,16,512]{3,2,1,0:T(8,128)(2,1)}, u32[]{:S(2)}, u32[]{:S(2)}) collective-permute-start(bf16[20,3,16,512]{3,2,1,0:T(8,128)(2,1)} %group_pack.32), channel_id=1, source_target_pairs={{0,16},{16,0},{1,17},{17,1},{2,18},{18,2},{3,19},{19,3},{4,20},{20... | collective-permute-start | bytes 2949128 | tf_op jit(solution)/shard_map/cond/branch_6_fun/ppermute | solution.py:412
  47.0 11.4 %collective-permute-start.111 = (bf16[4,3,64,512]{3,2,1,0:T(8,128)(2,1)}, bf16[4,3,64,512]{3,2,1,0:T(8,128)(2,1)}, u32[]{:S(2)}, u32[]{:S(2)}) collective-permute-start(bf16[4,3,64,512]{3,2,1,0:T(8,128)(2,1)} %get-tuple-element.631), channel_id=1, source_target_pairs={{0,3},{1,0},{2,1},{3,2},{4,7},{5,4},{6,5},{7,6},{8,11},{9,8},{10,9... | collective-permute-start | bytes 2359304 | tf_op jit(solution)/shard_map/cond/branch_6_fun/ppermute | solution.py:416
  47.8 25.4 %collective-permute-start.105 = (bf16[22,16,512]{2,1,0:T(8,128)(2,1)}, bf16[22,16,512]{2,1,0:T(8,128)(2,1)S(1)}, u32[]{:S(2)}, u32[]{:S(2)}) collective-permute-start(bf16[22,16,512]{2,1,0:T(8,128)(2,1)} %get-tuple-element.615), channel_id=1, source_target_pairs={{0,4},{1,5},{2,6},{3,7},{4,8},{5,9},{6,10},{7,11},{8,12},{9,13},{1... | collective-permute-start | bytes 1081352 | tf_op jit(solution)/shard_map/cond/branch_6_fun/ppermute | solution.py:409
  55.4 25.8 %collective-permute-start.106 = (bf16[22,16,512]{2,1,0:T(8,128)(2,1)}, bf16[22,16,512]{2,1,0:T(8,128)(2,1)}, u32[]{:S(2)}, u32[]{:S(2)}) collective-permute-start(bf16[22,16,512]{2,1,0:T(8,128)(2,1)} %get-tuple-element.616), channel_id=1, source_target_pairs={{0,8},{1,9},{2,10},{3,11},{4,12},{5,13},{6,14},{7,15},{8,0},{9,1},... | collective-permute-start | bytes 1081352 | tf_op jit(solution)/shard_map/cond/branch_6_fun/ppermute | solution.py:409
  56.8 24.4 %collective-permute-start.107 = (bf16[22,16,512]{2,1,0:T(8,128)(2,1)}, bf16[22,16,512]{2,1,0:T(8,128)(2,1)}, u32[]{:S(2)}, u32[]{:S(2)}) collective-permute-start(bf16[22,16,512]{2,1,0:T(8,128)(2,1)} %get-tuple-element.617), channel_id=1, source_target_pairs={{0,12},{1,13},{2,14},{3,15},{4,0},{5,1},{6,2},{7,3},{8,4},{9,5},{1... | collective-permute-start | bytes 1081352 | tf_op jit(solution)/shard_map/cond/branch_6_fun/ppermute | solution.py:409
  81.2 80.4 %all-to-all-start.6 = ((bf16[4,4,3,64,512]{4,3,2,1,0:T(8,128)(2,1)}), bf16[4,4,3,64,512]{4,3,2,1,0:T(8,128)(2,1)}, u32[]{:S(2)}, u32[]{:S(2)}) async-start(bf16[4,4,3,64,512]{4,3,2,1,0:T(8,128)(2,1)} %regroup.16), calls=%async_computation.6 | async-start | bytes 6291456 | tf_op jit(solution)/shard_map/cond/branch_6_fun/all_to_all | solution.py:445
  93.0 30.5 %copy-start.122 = (s32[16]{0:T(128)S(1)}, s32[16]{0:T(128)}, u32[]{:S(2)}) copy-start(s32[16]{0:T(128)} %get-tuple-element.837) | copy-start | bytes 196 | tf_op jit(solution)/shard_map/cond
  93.0 31.0 %copy-start.138 = (s32[64,1]{0,1:T(1,128)S(1)}, s32[64,1]{0,1:T(1,128)}, u32[]{:S(2)}) copy-start(s32[64,1]{0,1:T(1,128)} %get-tuple-element.913) | copy-start | bytes 772 | tf_op jit(solution)/shard_map/cond
  93.0 23.7 %collective-permute-start.115 = (bf16[20,3,16,512]{3,2,1,0:T(8,128)(2,1)}, bf16[20,3,16,512]{3,2,1,0:T(8,128)(2,1)}, u32[]{:S(2)}, u32[]{:S(2)}) collective-permute-start(bf16[20,3,16,512]{3,2,1,0:T(8,128)(2,1)} %group_pack.33), channel_id=1, source_target_pairs={{0,16},{16,0},{1,17},{17,1},{2,18},{18,2},{3,19},{19,3},{4,20},{20... | collective-permute-start | bytes 2949128 | tf_op jit(solution)/shard_map/cond/branch_6_fun/ppermute | solution.py:412
  93.6 28.5 %collective-permute-start.112 = (bf16[5,4,32,512]{3,2,1,0:T(8,128)(2,1)}, bf16[5,4,32,512]{3,2,1,0:T(8,128)(2,1)S(1)}, u32[]{:S(2)}, u32[]{:S(2)}) collective-permute-start(bf16[5,4,32,512]{3,2,1,0:T(8,128)(2,1)} %get-tuple-element.633), channel_id=1, source_target_pairs={{0,1},{1,2},{2,3},{3,0},{4,5},{5,6},{6,7},{7,4},{8,9},{9,10},{10,1... | collective-permute-start | bytes 1966088 | tf_op jit(solution)/shard_map/cond/branch_6_fun/ppermute | solution.py:416
  93.6 31.0 %collective-permute-start.113 = (bf16[5,4,32,512]{3,2,1,0:T(8,128)(2,1)}, bf16[5,4,32,512]{3,2,1,0:T(8,128)(2,1)S(1)}, u32[]{:S(2)}, u32[]{:S(2)}) collective-permute-start(bf16[5,4,32,512]{3,2,1,0:T(8,128)(2,1)} %get-tuple-element.634), channel_id=1, source_target_pairs={{0,2},{1,3},{2,0},{3,1},{4,6},{5,7},{6,4},{7,5},{8,10},{9,11},{10,... | collective-permute-start | bytes 1966088 | tf_op jit(solution)/shard_map/cond/branch_6_fun/ppermute | solution.py:416
  95.2 29.5 %collective-permute-start.114 = (bf16[5,4,32,512]{3,2,1,0:T(8,128)(2,1)}, bf16[5,4,32,512]{3,2,1,0:T(8,128)(2,1)}, u32[]{:S(2)}, u32[]{:S(2)}) collective-permute-start(bf16[5,4,32,512]{3,2,1,0:T(8,128)(2,1)} %get-tuple-element.635), channel_id=1, source_target_pairs={{0,3},{1,0},{2,1},{3,2},{4,7},{5,4},{6,5},{7,6},{8,11},{9,8},{10,9... | collective-permute-start | bytes 1966088 | tf_op jit(solution)/shard_map/cond/branch_6_fun/ppermute | solution.py:416
  120.4 18.0 %collective-permute-start.116 = (bf16[5,4,32,512]{3,2,1,0:T(8,128)(2,1)}, bf16[5,4,32,512]{3,2,1,0:T(8,128)(2,1)S(1)}, u32[]{:S(2)}, u32[]{:S(2)}) collective-permute-start(bf16[5,4,32,512]{3,2,1,0:T(8,128)(2,1)} %get-tuple-element.640), channel_id=1, source_target_pairs={{0,1},{1,2},{2,3},{3,0},{4,5},{5,6},{6,7},{7,4},{8,9},{9,10},{10,1... | collective-permute-start | bytes 1966088 | tf_op jit(solution)/shard_map/cond/branch_6_fun/ppermute | solution.py:416
  120.5 19.0 %collective-permute-start.117 = (bf16[5,4,32,512]{3,2,1,0:T(8,128)(2,1)}, bf16[5,4,32,512]{3,2,1,0:T(8,128)(2,1)S(1)}, u32[]{:S(2)}, u32[]{:S(2)}) collective-permute-start(bf16[5,4,32,512]{3,2,1,0:T(8,128)(2,1)} %get-tuple-element.641), channel_id=1, source_target_pairs={{0,2},{1,3},{2,0},{3,1},{4,6},{5,7},{6,4},{7,5},{8,10},{9,11},{10,... | collective-permute-start | bytes 1966088 | tf_op jit(solution)/shard_map/cond/branch_6_fun/ppermute | solution.py:416
  122.1 30.0 %copy-start.16 = (bf16[5,4,32,512]{3,2,1,0:T(8,128)(2,1)}, bf16[5,4,32,512]{3,2,1,0:T(8,128)(2,1)S(1)}, u32[]{:S(2)}) copy-start(bf16[5,4,32,512]{3,2,1,0:T(8,128)(2,1)S(1)} %collective-permute-done.112.rest_1_) | copy-start | bytes 1966084 | tf_op jit(solution)/shard_map/cond
  122.1 30.0 %collective-permute-start.118 = (bf16[5,4,32,512]{3,2,1,0:T(8,128)(2,1)}, bf16[5,4,32,512]{3,2,1,0:T(8,128)(2,1)S(1)}, u32[]{:S(2)}, u32[]{:S(2)}) collective-permute-start(bf16[5,4,32,512]{3,2,1,0:T(8,128)(2,1)} %get-tuple-element.642), channel_id=1, source_target_pairs={{0,3},{1,0},{2,1},{3,2},{4,7},{5,4},{6,5},{7,6},{8,11},{9,8},{10,9... | collective-permute-start | bytes 1966088 | tf_op jit(solution)/shard_map/cond/branch_6_fun/ppermute | solution.py:416
  124.6 27.5 %copy-start.26 = (bf16[5,4,32,512]{3,2,1,0:T(8,128)(2,1)}, bf16[5,4,32,512]{3,2,1,0:T(8,128)(2,1)S(1)}, u32[]{:S(2)}) copy-start(bf16[5,4,32,512]{3,2,1,0:T(8,128)(2,1)S(1)} %collective-permute-done.113.rest_2_) | copy-start | bytes 1966084 | tf_op jit(solution)/shard_map/cond
  (10 other events, 73.6 us)
where the time goes:
time: 172 us; the launch traced here: 168 us
  waiting for transfers between devices  85 us (49%)
  starting transfers between devices  39.1 us (23%)
  Pallas kernels  38.2 us (22%)
  local copies, waits for them, and re-layouts  3.89 us (2%)
    ppermute x2, waiting for transfers between devices, group_shift(): lax.ppermute(x, 'groups', [(i, (i + d) % groups) for i in range(groups)])  27.8 us
    ppermute x9, waiting for transfers between devices, shard_shift(): return lax.ppermute(x, 'blk', pairs)  27.5 us
    ppermute x6, waiting for transfers between devices, plane_shift(): lax.ppermute(x, 'blk', [(i, (i + s * PLANE) % devices) for i in range(dev...  25 us
    ppermute x6, starting transfers between devices, plane_shift(): lax.ppermute(x, 'blk', [(i, (i + s * PLANE) % devices) for i in range(dev...  16.1 us
    all_to_all x1, starting transfers between devices, branch(): lax.all_to_all(up_packed, 'blk', split_axis=0, concat_axis=0, tiled=True,...  9.57 us
    ppermute x9, starting transfers between devices, shard_shift(): return lax.ppermute(x, 'blk', pairs)  8.36 us
    pallas_call x2, Pallas kernels, shard_pack(): pl.pallas_call(functools.partial(shard_pack_kernel, dims, first), out_sha...  7.43 us
    pallas_call x1, Pallas kernels, expand(): pl.pallas_call(expand_kernel, grid=(own,), out_shape=jax.ShapeDtypeStruct...  6.44 us
  transfers between devices with their start and end apart: 19, of which 10 were waited for; matrix products, arithmetic and copies ran while one was open for 1% of the time, Pallas kernels for 14%

commit v1 on v0

--- a/solution.py
+++ b/solution.py
@@ -326,7 +326,7 @@
             *[pl.BlockSpec((1, planes, ranks, width), lambda b: (b, 0, 0, 0))] * len(maps),
         ],
         out_specs=pl.BlockSpec((BLOCK, rank), lambda b: (b, 0)),
-        compiler_params=pltpu.CompilerParams(vmem_limit_bytes=VMEM_BYTES),
+        compiler_params=pltpu.CompilerParams(vmem_limit_bytes=VMEM_BYTES // 2),
         cost_estimate=SMALL,
         name="shrink",
     )(where, tokens, *maps)

time: 172 us -> 166 us (0.965); the launches traced: 168 us -> 168 us
  transfers between devices with their start and end apart: 19 -> 19, of which waited for: 10 -> 10; matrix products, arithmetic and copies ran while one was open for 1% -> 1% of each run, Pallas kernels for 14% -> 13%
where the time goes in v1:
time: 166 us; the launch traced here: 168 us
  waiting for transfers between devices  84.5 us (51%)
  starting transfers between devices  39.1 us (24%)
  Pallas kernels  37.6 us (23%)
  local copies, waits for them, and re-layouts  4.89 us (3%)
    ppermute x2, waiting for transfers between devices, group_shift(): lax.ppermute(x, 'groups', [(i, (i + d) % groups) for i in range(groups)])  27.8 us
    ppermute x9, waiting for transfers between devices, shard_shift(): return lax.ppermute(x, 'blk', pairs)  26.8 us
    ppermute x6, waiting for transfers between devices, plane_shift(): lax.ppermute(x, 'blk', [(i, (i + s * PLANE) % devices) for i in range(dev...  24.9 us
    ppermute x6, starting transfers between devices, plane_shift(): lax.ppermute(x, 'blk', [(i, (i + s * PLANE) % devices) for i in range(dev...  16.1 us
    all_to_all x1, starting transfers between devices, branch(): lax.all_to_all(up_packed, 'blk', split_axis=0, concat_axis=0, tiled=True,...  9.57 us
    ppermute x9, starting transfers between devices, shard_shift(): return lax.ppermute(x, 'blk', pairs)  8.36 us
    pallas_call x2, Pallas kernels, shard_pack(): pl.pallas_call(functools.partial(shard_pack_kernel, dims, first), out_sha...  8.06 us
    pallas_call x1, Pallas kernels, expand(): pl.pallas_call(expand_kernel, grid=(own,), out_shape=jax.ShapeDtypeStruct...  6.5 us
  transfers between devices with their start and end apart: 19, of which 10 were waited for; matrix products, arithmetic and copies ran while one was open for 1% of the time, Pallas kernels for 13%

profile of v1, /device:TPU:0, one launch (start us, length us, event | category | flops | bytes accessed | tf_op | source)
XLA Modules:
  0.0 168.3 jit_solution(3509219985661543613)
XLA Ops:
  0.7 2.9 %collective-permute-start.170 = (s32[80]{0:T(128)S(1)}, s32[80]{0:T(128)S(1)}, u32[]{:S(2)}, u32[]{:S(2)}) collective-permute-start(s32[80]{0:T(128)S(1)} %pad_add_fusion.1.rest_0_), channel_id=1, source_target_pairs={{0,16},{16,0},{1,17},{17,1},{2,18},{18,2},{3,19},{19,3},{4,20},{20... | collective-permute-start | bytes 968 | tf_op jit(solution)/shard_map/ppermute | solution.py:401
  5.7 5.8 %prepare.1 = (bf16[4,3,64,512]{3,2,1,0:T(8,128)(2,1)S(1)}, bf16[4,3,64,512]{3,2,1,0:T(8,128)(2,1)}, bf16[4,3,64,512]{3,2,1,0:T(8,128)(2,1)}, bf16[4,3,64,512]{3,...) custom-call(s32[3]{0:T(128)S(1)} %pad_add_fusion.where, ...), custom_call_target="tpu_custom_call" | custom-call | bytes 1024 | tf_op jit(solution)/shard_map/prepare/pallas_call | solution.py:121
  12.2 156.0 %conditional.1 = (bf16[256,8192]{1,0:T(8,128)(2,1)}) conditional(s32[]{:T(128)} %bitcast.24, (s32[3]{0:T(128)S(1)}, s32[164]{0:T(256)S(1)}, s32[4]{0:T(128)S(1)}, bf16[32,64,512]{2,1,0:T(8,128)(2,1)}, bf16[32,64,512]{2,1,0:T(8,128)(2,1)}, /*index=5*/s32[32]{0:T(128)S(1)}, s32[8]{0:T(128)S(1)}, s32[64,1]{0,1:T(1,128)}, ...), branch_computations={%region_0.1_spmd, %region_1.2_spmd, %region_2.3_spmd, %region_3.4_... | conditional | flops 8 | bytes 83243120 | solution.py:454
  12.4 2.8 %plane_pack.32 = (bf16[22,16,512]{2,1,0:T(8,128)(2,1)}, bf16[22,16,512]{2,1,0:T(8,128)(2,1)}, bf16[22,16,512]{2,1,0:T(8,128)(2,1)}) custom-call(s32[3]{0:T(128)S(1)} %get-tuple-element.600.where, s32[164]{0:T(256)S(1)} %get-tuple-element.605.lists, s32[4]{0:T(128)S(1)} %get-tuple-element.606.bounds, bf16[32,64,512]{2,1,0:T(8,128)(2,1)} %get-tuple-element.607.panels, ...), custom_call_target="tpu_custom_call" | custom-call | bytes 1024 | tf_op jit(solution)/shard_map/cond/branch_6_fun/plane_pack/pallas_call | solution.py:195
  15.3 2.2 %collective-permute-start.102 = (bf16[22,16,512]{2,1,0:T(8,128)(2,1)}, bf16[22,16,512]{2,1,0:T(8,128)(2,1)S(1)}, u32[]{:S(2)}, u32[]{:S(2)}) collective-permute-start(bf16[22,16,512]{2,1,0:T(8,128)(2,1)} %get-tuple-element.609), channel_id=1, source_target_pairs={{0,4},{1,5},{2,6},{3,7},{4,8},{5,9},{6,10},{7,11},{8,12},{9,13},{1... | collective-permute-start | bytes 1081352 | tf_op jit(solution)/shard_map/cond/branch_6_fun/ppermute | solution.py:409
  17.4 2.6 %collective-permute-start.103 = (bf16[22,16,512]{2,1,0:T(8,128)(2,1)}, bf16[22,16,512]{2,1,0:T(8,128)(2,1)S(1)}, u32[]{:S(2)}, u32[]{:S(2)}) collective-permute-start(bf16[22,16,512]{2,1,0:T(8,128)(2,1)} %get-tuple-element.610), channel_id=1, source_target_pairs={{0,8},{1,9},{2,10},{3,11},{4,12},{5,13},{6,14},{7,15},{8,0},{9,1},... | collective-permute-start | bytes 1081352 | tf_op jit(solution)/shard_map/cond/branch_6_fun/ppermute | solution.py:409
  22.9 2.7 %plane_pack.33 = (bf16[22,16,512]{2,1,0:T(8,128)(2,1)}, bf16[22,16,512]{2,1,0:T(8,128)(2,1)}, bf16[22,16,512]{2,1,0:T(8,128)(2,1)}) custom-call(s32[3]{0:T(128)S(1)} %get-tuple-element.600.where, s32[164]{0:T(256)S(1)} %get-tuple-element.605.lists, s32[4]{0:T(128)S(1)} %get-tuple-element.606.bounds, bf16[32,64,512]{2,1,0:T(8,128)(2,1)} %get-tuple-element.607.panels, ...), custom_call_target="tpu_custom_call" | custom-call | bytes 1024 | tf_op jit(solution)/shard_map/cond/branch_6_fun/plane_pack/pallas_call | solution.py:195
  25.6 3.5 %collective-permute-done.102.rest_0_ = bf16[22,16,512]{2,1,0:T(8,128)(2,1)S(1)} collective-permute-done((bf16[22,16,512]{2,1,0:T(8,128)(2,1)}, bf16[22,16,512]{2,1,0:T(8,128)(2,1)S(1)}, u32[]{:S(2)}, u32[]{:S(2)}) %collective-permute-start.102) | collective-permute-done | bytes 360480 | tf_op jit(solution)/shard_map/cond/branch_6_fun/ppermute | solution.py:409
  29.1 13.4 %collective-permute-done.103.rest_1_ = bf16[22,16,512]{2,1,0:T(8,128)(2,1)S(1)} collective-permute-done((bf16[22,16,512]{2,1,0:T(8,128)(2,1)}, bf16[22,16,512]{2,1,0:T(8,128)(2,1)S(1)}, u32[]{:S(2)}, u32[]{:S(2)}) %collective-permute-start.103) | collective-permute-done | bytes 360480 | tf_op jit(solution)/shard_map/cond/branch_6_fun/ppermute | solution.py:409
  43.3 2.2 %group_pack.32 = bf16[20,3,16,512]{3,2,1,0:T(8,128)(2,1)} custom-call(s32[3]{0:T(128)S(1)} %get-tuple-element.600.where, s32[32]{0:T(128)S(1)} %get-tuple-element.618.places, s32[8]{0:T(128)S(1)} %get-tuple-element.619.last_places, bf16[22,16,512]{2,1,0:T(8,128)(2,1)} %copy-done.87, bf16[22,16,512]{2,1,0:T(8,128)(2,1)} %copy-done.88, ...), custom_call_target="tpu_custom_call" | custom-call | bytes 1024 | tf_op jit(solution)/shard_map/cond/branch_6_fun/group_pack/pallas_call | solution.py:237
  47.8 7.7 %collective-permute-start.105 = (bf16[22,16,512]{2,1,0:T(8,128)(2,1)}, bf16[22,16,512]{2,1,0:T(8,128)(2,1)S(1)}, u32[]{:S(2)}, u32[]{:S(2)}) collective-permute-start(bf16[22,16,512]{2,1,0:T(8,128)(2,1)} %get-tuple-element.615), channel_id=1, source_target_pairs={{0,4},{1,5},{2,6},{3,7},{4,8},{5,9},{6,10},{7,11},{8,12},{9,13},{1... | collective-permute-start | bytes 1081352 | tf_op jit(solution)/shard_map/cond/branch_6_fun/ppermute | solution.py:409
  58.4 3.3 %regroup.16 = bf16[4,4,3,64,512]{4,3,2,1,0:T(8,128)(2,1)} custom-call(s32[3]{0:T(128)S(1)} %get-tuple-element.600.where, bf16[4,3,64,512]{3,2,1,0:T(8,128)(2,1)S(1)} %get-tuple-element.628.refs_0_, bf16[4,3,64,512]{3,2,1,0:T(8,128)(2,1)} %collective-permute-done.109.refs_1_, bf16[4,3,64,512]{3,2,1,0:T(8,128)(2,1)} %collective-permute-done.110.refs_2_, ...), custom_call_target="tpu_custom_call" | custom-call | bytes 1024 | tf_op jit(solution)/shard_map/cond/branch_6_fun/regroup/pallas_call | solution.py:150
  61.7 7.7 %collective-permute-done.108.rest_3_ = bf16[20,3,16,512]{3,2,1,0:T(8,128)(2,1)} collective-permute-done((bf16[20,3,16,512]{3,2,1,0:T(8,128)(2,1)}, bf16[20,3,16,512]{3,2,1,0:T(8,128)(2,1)}, u32[]{:S(2)}, u32[]{:S(2)}) %collective-permute-start.108) | collective-permute-done | bytes 983072 | tf_op jit(solution)/shard_map/cond/branch_6_fun/ppermute | solution.py:412
  69.4 3.7 %shard_pack.32 = (bf16[5,4,32,512]{3,2,1,0:T(8,128)(2,1)}, bf16[5,4,32,512]{3,2,1,0:T(8,128)(2,1)}, bf16[5,4,32,512]{3,2,1,0:T(8,128)(2,1)}, bf16[5,4,32,512]{3,2,1,0:T(8,128)(2,1)}) custom-call(s32[3]{0:T(128)S(1)} %get-tuple-element.600.where, s32[32]{0:T(128)S(1)} %get-tuple-element.618.places, s32[8]{0:T(128)S(1)} %get-tuple-element.619.last_places, ...), custom_call_target="tpu_custom_call" | custom-call | bytes 1024 | tf_op jit(solution)/shard_map/cond/branch_6_fun/shard_pack/pallas_call | solution.py:287
  73.2 8.0 %collective-permute-done.106.rest_1_ = bf16[22,16,512]{2,1,0:T(8,128)(2,1)} collective-permute-done((bf16[22,16,512]{2,1,0:T(8,128)(2,1)}, bf16[22,16,512]{2,1,0:T(8,128)(2,1)}, u32[]{:S(2)}, u32[]{:S(2)}) %collective-permute-start.106) | collective-permute-done | bytes 360480 | tf_op jit(solution)/shard_map/cond/branch_6_fun/ppermute | solution.py:409
  81.2 9.6 %all-to-all-start.6 = ((bf16[4,4,3,64,512]{4,3,2,1,0:T(8,128)(2,1)}), bf16[4,4,3,64,512]{4,3,2,1,0:T(8,128)(2,1)}, u32[]{:S(2)}, u32[]{:S(2)}) async-start(bf16[4,4,3,64,512]{4,3,2,1,0:T(8,128)(2,1)} %regroup.16), calls=%async_computation.6 | async-start | bytes 6291456 | tf_op jit(solution)/shard_map/cond/branch_6_fun/all_to_all | solution.py:445
  90.8 2.2 %group_pack.33 = bf16[20,3,16,512]{3,2,1,0:T(8,128)(2,1)} custom-call(s32[3]{0:T(128)S(1)} %get-tuple-element.600.where, s32[32]{0:T(128)S(1)} %get-tuple-element.618.places, s32[8]{0:T(128)S(1)} %get-tuple-element.619.last_places, bf16[22,16,512]{2,1,0:T(8,128)(2,1)} %copy-done.86, bf16[22,16,512]{2,1,0:T(8,128)(2,1)} %collective-permute-done.106.rest_1_, ...), custom_call_target="tpu_custom_call" | custom-call | bytes 1024 | tf_op jit(solution)/shard_map/cond/branch_6_fun/group_pack/pallas_call | solution.py:237
  96.6 20.1 %collective-permute-done.115.rest_3_ = bf16[20,3,16,512]{3,2,1,0:T(8,128)(2,1)} collective-permute-done((bf16[20,3,16,512]{3,2,1,0:T(8,128)(2,1)}, bf16[20,3,16,512]{3,2,1,0:T(8,128)(2,1)}, u32[]{:S(2)}, u32[]{:S(2)}) %collective-permute-start.115) | collective-permute-done | bytes 983072 | tf_op jit(solution)/shard_map/cond/branch_6_fun/ppermute | solution.py:412
  116.7 4.3 %shard_pack.33 = (bf16[5,4,32,512]{3,2,1,0:T(8,128)(2,1)}, bf16[5,4,32,512]{3,2,1,0:T(8,128)(2,1)}, bf16[5,4,32,512]{3,2,1,0:T(8,128)(2,1)}, bf16[5,4,32,512]{3,2,1,0:T(8,128)(2,1)}) custom-call(s32[3]{0:T(128)S(1)} %get-tuple-element.600.where, s32[32]{0:T(128)S(1)} %get-tuple-element.618.places, s32[8]{0:T(128)S(1)} %get-tuple-element.619.last_places, ...), custom_call_target="tpu_custom_call" | custom-call | bytes 1024 | tf_op jit(solution)/shard_map/cond/branch_6_fun/shard_pack/pallas_call | solution.py:287
  125.4 13.0 %collective-permute-done.116.rest_5_ = bf16[5,4,32,512]{3,2,1,0:T(8,128)(2,1)S(1)} collective-permute-done((bf16[5,4,32,512]{3,2,1,0:T(8,128)(2,1)}, bf16[5,4,32,512]{3,2,1,0:T(8,128)(2,1)S(1)}, u32[]{:S(2)}, u32[]{:S(2)}) %collective-permute-start.116) | collective-permute-done | bytes 655392 | tf_op jit(solution)/shard_map/cond/branch_6_fun/ppermute | solution.py:416
  139.6 12.5 %collective-permute-done.118.rest_7_ = bf16[5,4,32,512]{3,2,1,0:T(8,128)(2,1)} collective-permute-done((bf16[5,4,32,512]{3,2,1,0:T(8,128)(2,1)}, bf16[5,4,32,512]{3,2,1,0:T(8,128)(2,1)}, u32[]{:S(2)}, u32[]{:S(2)}) %collective-permute-start.118) | collective-permute-done | bytes 655392 | tf_op jit(solution)/shard_map/cond/branch_6_fun/ppermute | solution.py:416
  153.3 4.1 %shrink.16.shrunk = bf16[256,64]{1,0:T(8,128)(2,1)S(1)} custom-call(s32[3]{0:T(128)S(1)} %get-tuple-element.600.where, bf16[256,8192]{1,0:T(8,128)(2,1)} %get-tuple-element.891.tokens, bf16[5,4,32,512]{3,2,1,0:T(8,128)(2,1)S(1)} %copy-done.6, bf16[5,4,32,512]{3,2,1,0:T(8,128)(2,1)S(1)} %collective-permute-done.112.rest_1_, ...), custom_call_target="tpu_custom_call" | custom-call | bytes 1024 | tf_op jit(solution)/shard_map/cond/branch_6_fun/shrink/pallas_call | solution.py:319
  158.1 3.6 %all-to-all-done.6.direct = bf16[4,4,3,64,512]{4,3,2,1,0:T(8,128)(2,1)} async-done(((bf16[4,4,3,64,512]{4,3,2,1,0:T(8,128)(2,1)}), bf16[4,4,3,64,512]{4,3,2,1,0:T(8,128)(2,1)}, u32[]{:S(2)}, u32[]{:S(2)}) %all-to-all-start.6) | async-done | bytes 3145760 | tf_op jit(solution)/shard_map/cond/branch_6_fun/all_to_all | solution.py:445
  161.6 6.5 %expand.16 = bf16[256,8192]{1,0:T(8,128)(2,1)} custom-call(s32[3]{0:T(128)S(1)} %get-tuple-element.600.where, s32[4]{0:T(128)} %fusion.12.ids, s32[1]{0:T(128)} %dynamic_slice.44.count, f32[32]{0:T(128)S(1)} %copy-done.116, bf16[256,64]{1,0:T(8,128)(2,1)} %copy-done.66, bf16[4,4,3,64,512]{4,3,2,1,0:T(8,128)(2,1)} %all-to-all-done.6.direct, ...), custom_call_target="tpu_custom_call" | custom-call | bytes 1024 | tf_op jit(solution)/shard_map/cond/branch_6_fun/expand/pallas_call | solution.py:367
  (62 shorter events, 22.6 us)
Async XLA Ops:
  0.7 4.5 %collective-permute-start.170 = (s32[80]{0:T(128)S(1)}, s32[80]{0:T(128)S(1)}, u32[]{:S(2)}, u32[]{:S(2)}) collective-permute-start(s32[80]{0:T(128)S(1)} %pad_add_fusion.1.rest_0_), channel_id=1, source_target_pairs={{0,16},{16,0},{1,17},{17,1},{2,18},{18,2},{3,19},{19,3},{4,20},{20... | collective-permute-start | bytes 968 | tf_op jit(solution)/shard_map/ppermute | solution.py:401
  15.3 13.9 %collective-permute-start.102 = (bf16[22,16,512]{2,1,0:T(8,128)(2,1)}, bf16[22,16,512]{2,1,0:T(8,128)(2,1)S(1)}, u32[]{:S(2)}, u32[]{:S(2)}) collective-permute-start(bf16[22,16,512]{2,1,0:T(8,128)(2,1)} %get-tuple-element.609), channel_id=1, source_target_pairs={{0,4},{1,5},{2,6},{3,7},{4,8},{5,9},{6,10},{7,11},{8,12},{9,13},{1... | collective-permute-start | bytes 1081352 | tf_op jit(solution)/shard_map/cond/branch_6_fun/ppermute | solution.py:409
  17.4 25.1 %collective-permute-start.103 = (bf16[22,16,512]{2,1,0:T(8,128)(2,1)}, bf16[22,16,512]{2,1,0:T(8,128)(2,1)S(1)}, u32[]{:S(2)}, u32[]{:S(2)}) collective-permute-start(bf16[22,16,512]{2,1,0:T(8,128)(2,1)} %get-tuple-element.610), channel_id=1, source_target_pairs={{0,8},{1,9},{2,10},{3,11},{4,12},{5,13},{6,14},{7,15},{8,0},{9,1},... | collective-permute-start | bytes 1081352 | tf_op jit(solution)/shard_map/cond/branch_6_fun/ppermute | solution.py:409
  20.0 22.5 %collective-permute-start.104 = (bf16[22,16,512]{2,1,0:T(8,128)(2,1)}, bf16[22,16,512]{2,1,0:T(8,128)(2,1)}, u32[]{:S(2)}, u32[]{:S(2)}) collective-permute-start(bf16[22,16,512]{2,1,0:T(8,128)(2,1)} %get-tuple-element.611), channel_id=1, source_target_pairs={{0,12},{1,13},{2,14},{3,15},{4,0},{5,1},{6,2},{7,3},{8,4},{9,5},{1... | collective-permute-start | bytes 1081352 | tf_op jit(solution)/shard_map/cond/branch_6_fun/ppermute | solution.py:409
  21.4 34.1 %collective-permute-start.109 = (bf16[4,3,64,512]{3,2,1,0:T(8,128)(2,1)}, bf16[4,3,64,512]{3,2,1,0:T(8,128)(2,1)}, u32[]{:S(2)}, u32[]{:S(2)}) collective-permute-start(bf16[4,3,64,512]{3,2,1,0:T(8,128)(2,1)} %get-tuple-element.629), channel_id=1, source_target_pairs={{0,1},{1,2},{2,3},{3,0},{4,5},{5,6},{6,7},{7,4},{8,9},{9,10},{10,1... | collective-permute-start | bytes 2359304 | tf_op jit(solution)/shard_map/cond/branch_6_fun/ppermute | solution.py:416
  21.4 36.4 %copy-start.138 = (s32[64,1]{0,1:T(1,128)S(1)}, s32[64,1]{0,1:T(1,128)}, u32[]{:S(2)}) copy-start(s32[64,1]{0,1:T(1,128)} %get-tuple-element.913) | copy-start | bytes 772 | tf_op jit(solution)/shard_map/cond
  21.4 35.4 %collective-permute-start.110 = (bf16[4,3,64,512]{3,2,1,0:T(8,128)(2,1)}, bf16[4,3,64,512]{3,2,1,0:T(8,128)(2,1)}, u32[]{:S(2)}, u32[]{:S(2)}) collective-permute-start(bf16[4,3,64,512]{3,2,1,0:T(8,128)(2,1)} %get-tuple-element.630), channel_id=1, source_target_pairs={{0,2},{1,3},{2,0},{3,1},{4,6},{5,7},{6,4},{7,5},{8,10},{9,11},{10,... | collective-permute-start | bytes 2359304 | tf_op jit(solution)/shard_map/cond/branch_6_fun/ppermute | solution.py:416
  45.5 24.0 %collective-permute-start.108 = (bf16[20,3,16,512]{3,2,1,0:T(8,128)(2,1)}, bf16[20,3,16,512]{3,2,1,0:T(8,128)(2,1)}, u32[]{:S(2)}, u32[]{:S(2)}) collective-permute-start(bf16[20,3,16,512]{3,2,1,0:T(8,128)(2,1)} %group_pack.32), channel_id=1, source_target_pairs={{0,16},{16,0},{1,17},{17,1},{2,18},{18,2},{3,19},{19,3},{4,20},{20... | collective-permute-start | bytes 2949128 | tf_op jit(solution)/shard_map/cond/branch_6_fun/ppermute | solution.py:412
  47.0 11.4 %collective-permute-start.111 = (bf16[4,3,64,512]{3,2,1,0:T(8,128)(2,1)}, bf16[4,3,64,512]{3,2,1,0:T(8,128)(2,1)}, u32[]{:S(2)}, u32[]{:S(2)}) collective-permute-start(bf16[4,3,64,512]{3,2,1,0:T(8,128)(2,1)} %get-tuple-element.631), channel_id=1, source_target_pairs={{0,3},{1,0},{2,1},{3,2},{4,7},{5,4},{6,5},{7,6},{8,11},{9,8},{10,9... | collective-permute-start | bytes 2359304 | tf_op jit(solution)/shard_map/cond/branch_6_fun/ppermute | solution.py:416
  47.8 25.4 %collective-permute-start.105 = (bf16[22,16,512]{2,1,0:T(8,128)(2,1)}, bf16[22,16,512]{2,1,0:T(8,128)(2,1)S(1)}, u32[]{:S(2)}, u32[]{:S(2)}) collective-permute-start(bf16[22,16,512]{2,1,0:T(8,128)(2,1)} %get-tuple-element.615), channel_id=1, source_target_pairs={{0,4},{1,5},{2,6},{3,7},{4,8},{5,9},{6,10},{7,11},{8,12},{9,13},{1... | collective-permute-start | bytes 1081352 | tf_op jit(solution)/shard_map/cond/branch_6_fun/ppermute | solution.py:409
  55.4 25.8 %collective-permute-start.106 = (bf16[22,16,512]{2,1,0:T(8,128)(2,1)}, bf16[22,16,512]{2,1,0:T(8,128)(2,1)}, u32[]{:S(2)}, u32[]{:S(2)}) collective-permute-start(bf16[22,16,512]{2,1,0:T(8,128)(2,1)} %get-tuple-element.616), channel_id=1, source_target_pairs={{0,8},{1,9},{2,10},{3,11},{4,12},{5,13},{6,14},{7,15},{8,0},{9,1},... | collective-permute-start | bytes 1081352 | tf_op jit(solution)/shard_map/cond/branch_6_fun/ppermute | solution.py:409
  56.8 24.4 %collective-permute-start.107 = (bf16[22,16,512]{2,1,0:T(8,128)(2,1)}, bf16[22,16,512]{2,1,0:T(8,128)(2,1)}, u32[]{:S(2)}, u32[]{:S(2)}) collective-permute-start(bf16[22,16,512]{2,1,0:T(8,128)(2,1)} %get-tuple-element.617), channel_id=1, source_target_pairs={{0,12},{1,13},{2,14},{3,15},{4,0},{5,1},{6,2},{7,3},{8,4},{9,5},{1... | collective-permute-start | bytes 1081352 | tf_op jit(solution)/shard_map/cond/branch_6_fun/ppermute | solution.py:409
  81.2 80.4 %all-to-all-start.6 = ((bf16[4,4,3,64,512]{4,3,2,1,0:T(8,128)(2,1)}), bf16[4,4,3,64,512]{4,3,2,1,0:T(8,128)(2,1)}, u32[]{:S(2)}, u32[]{:S(2)}) async-start(bf16[4,4,3,64,512]{4,3,2,1,0:T(8,128)(2,1)} %regroup.16), calls=%async_computation.6 | async-start | bytes 6291456 | tf_op jit(solution)/shard_map/cond/branch_6_fun/all_to_all | solution.py:445
  93.0 59.1 %copy-start.6 = (bf16[5,4,32,512]{3,2,1,0:T(8,128)(2,1)S(1)}, bf16[5,4,32,512]{3,2,1,0:T(8,128)(2,1)}, u32[]{:S(2)}) copy-start(bf16[5,4,32,512]{3,2,1,0:T(8,128)(2,1)} %get-tuple-element.632.rest_0_) | copy-start | bytes 1966084 | tf_op jit(solution)/shard_map/cond
  93.0 23.7 %collective-permute-start.115 = (bf16[20,3,16,512]{3,2,1,0:T(8,128)(2,1)}, bf16[20,3,16,512]{3,2,1,0:T(8,128)(2,1)}, u32[]{:S(2)}, u32[]{:S(2)}) collective-permute-start(bf16[20,3,16,512]{3,2,1,0:T(8,128)(2,1)} %group_pack.33), channel_id=1, source_target_pairs={{0,16},{16,0},{1,17},{17,1},{2,18},{18,2},{3,19},{19,3},{4,20},{20... | collective-permute-start | bytes 2949128 | tf_op jit(solution)/shard_map/cond/branch_6_fun/ppermute | solution.py:412
  93.6 29.1 %collective-permute-start.112 = (bf16[5,4,32,512]{3,2,1,0:T(8,128)(2,1)}, bf16[5,4,32,512]{3,2,1,0:T(8,128)(2,1)S(1)}, u32[]{:S(2)}, u32[]{:S(2)}) collective-permute-start(bf16[5,4,32,512]{3,2,1,0:T(8,128)(2,1)} %get-tuple-element.633), channel_id=1, source_target_pairs={{0,1},{1,2},{2,3},{3,0},{4,5},{5,6},{6,7},{7,4},{8,9},{9,10},{10,1... | collective-permute-start | bytes 1966088 | tf_op jit(solution)/shard_map/cond/branch_6_fun/ppermute | solution.py:416
  93.6 31.7 %collective-permute-start.113 = (bf16[5,4,32,512]{3,2,1,0:T(8,128)(2,1)}, bf16[5,4,32,512]{3,2,1,0:T(8,128)(2,1)S(1)}, u32[]{:S(2)}, u32[]{:S(2)}) collective-permute-start(bf16[5,4,32,512]{3,2,1,0:T(8,128)(2,1)} %get-tuple-element.634), channel_id=1, source_target_pairs={{0,2},{1,3},{2,0},{3,1},{4,6},{5,7},{6,4},{7,5},{8,10},{9,11},{10,... | collective-permute-start | bytes 1966088 | tf_op jit(solution)/shard_map/cond/branch_6_fun/ppermute | solution.py:416
  95.2 30.2 %collective-permute-start.114 = (bf16[5,4,32,512]{3,2,1,0:T(8,128)(2,1)}, bf16[5,4,32,512]{3,2,1,0:T(8,128)(2,1)S(1)}, u32[]{:S(2)}, u32[]{:S(2)}) collective-permute-start(bf16[5,4,32,512]{3,2,1,0:T(8,128)(2,1)} %get-tuple-element.635), channel_id=1, source_target_pairs={{0,3},{1,0},{2,1},{3,2},{4,7},{5,4},{6,5},{7,6},{8,11},{9,8},{10,9... | collective-permute-start | bytes 1966088 | tf_op jit(solution)/shard_map/cond/branch_6_fun/ppermute | solution.py:416
  121.0 17.4 %collective-permute-start.116 = (bf16[5,4,32,512]{3,2,1,0:T(8,128)(2,1)}, bf16[5,4,32,512]{3,2,1,0:T(8,128)(2,1)S(1)}, u32[]{:S(2)}, u32[]{:S(2)}) collective-permute-start(bf16[5,4,32,512]{3,2,1,0:T(8,128)(2,1)} %get-tuple-element.640), channel_id=1, source_target_pairs={{0,1},{1,2},{2,3},{3,0},{4,5},{5,6},{6,7},{7,4},{8,9},{9,10},{10,1... | collective-permute-start | bytes 1966088 | tf_op jit(solution)/shard_map/cond/branch_6_fun/ppermute | solution.py:416
  121.1 18.5 %collective-permute-start.117 = (bf16[5,4,32,512]{3,2,1,0:T(8,128)(2,1)}, bf16[5,4,32,512]{3,2,1,0:T(8,128)(2,1)}, u32[]{:S(2)}, u32[]{:S(2)}) collective-permute-start(bf16[5,4,32,512]{3,2,1,0:T(8,128)(2,1)} %get-tuple-element.641), channel_id=1, source_target_pairs={{0,2},{1,3},{2,0},{3,1},{4,6},{5,7},{6,4},{7,5},{8,10},{9,11},{10,... | collective-permute-start | bytes 1966088 | tf_op jit(solution)/shard_map/cond/branch_6_fun/ppermute | solution.py:416
  122.7 34.7 %copy-start.16 = (bf16[5,4,32,512]{3,2,1,0:T(8,128)(2,1)}, bf16[5,4,32,512]{3,2,1,0:T(8,128)(2,1)S(1)}, u32[]{:S(2)}) copy-start(bf16[5,4,32,512]{3,2,1,0:T(8,128)(2,1)S(1)} %collective-permute-done.112.rest_1_) | copy-start | bytes 1966084 | tf_op jit(solution)/shard_map/cond
  122.7 29.5 %collective-permute-start.118 = (bf16[5,4,32,512]{3,2,1,0:T(8,128)(2,1)}, bf16[5,4,32,512]{3,2,1,0:T(8,128)(2,1)}, u32[]{:S(2)}, u32[]{:S(2)}) collective-permute-start(bf16[5,4,32,512]{3,2,1,0:T(8,128)(2,1)} %get-tuple-element.642), channel_id=1, source_target_pairs={{0,3},{1,0},{2,1},{3,2},{4,7},{5,4},{6,5},{7,6},{8,11},{9,8},{10,9... | collective-permute-start | bytes 1966088 | tf_op jit(solution)/shard_map/cond/branch_6_fun/ppermute | solution.py:416
  125.4 32.0 %copy-start.26 = (bf16[5,4,32,512]{3,2,1,0:T(8,128)(2,1)}, bf16[5,4,32,512]{3,2,1,0:T(8,128)(2,1)S(1)}, u32[]{:S(2)}) copy-start(bf16[5,4,32,512]{3,2,1,0:T(8,128)(2,1)S(1)} %collective-permute-done.113.rest_2_) | copy-start | bytes 1966084 | tf_op jit(solution)/shard_map/cond
  125.4 32.0 %copy-start.36 = (bf16[5,4,32,512]{3,2,1,0:T(8,128)(2,1)}, bf16[5,4,32,512]{3,2,1,0:T(8,128)(2,1)S(1)}, u32[]{:S(2)}) copy-start(bf16[5,4,32,512]{3,2,1,0:T(8,128)(2,1)S(1)} %collective-permute-done.114.rest_3_) | copy-start | bytes 1966084 | tf_op jit(solution)/shard_map/cond
  (11 other events, 97.8 us)
